TPU v7x, 32 devices: a whole 2x2x4 slice. The times are simulated.
32 devices in a mesh: leaf: 4 (over y, x), box: 8 (over z, core).
Axes of the slice: x: 2, y: 2, z: 4, core: 2. Of those that a mesh axis runs over, the one named last changes fastest.
Arguments:
- krylov_block: float32 [64, 32768], P(None, ('leaf', 'box')), as said below
- bases: float32 [32, 32768], P(None, ('leaf', 'box')), may hold values from -0.5 to 0.5
- points: float32 [3, 32768], P(None, ('leaf', 'box')), may hold values from 0 to 1, as said below
- panel_size: float32 [32768], P(('leaf', 'box')), may hold values from 0.002 to 0.008
- panel_weight: float32 [32768], P(('leaf', 'box')), may hold values from 0.5 to 2
- near_list: int32 [256, 16], P(('leaf', 'box')), may hold values from 0 to 255, as said below
- far_list: int32 [256, 12], P(('leaf', 'box')), may hold values from 0 to 255, as said below
- far_class: int32 [256, 12], P(('leaf', 'box')), may hold values from 0 to 15
- far_count: int32 [256], P(('leaf', 'box')), may hold values from 1 to 12
- coarse_list: int32 [32, 16], P(('leaf', 'box')), may hold values from 0 to 31, as said below
- coarse_class: int32 [32, 16], P(('leaf', 'box')), may hold values from 0 to 15
- coarse_count: int32 [32], P(('leaf', 'box')), may hold values from 1 to 16
- couple_fine: float32 [16, 32, 32], replicated, may hold values from -0.3125 to 0.3125
- couple_coarse: float32 [16, 32, 32], replicated, may hold values from -1 to 1
- up_transfer: float32 [8, 32, 32], replicated, may hold values from -0.375 to 0.375
- down_transfer: float32 [8, 32, 32], replicated, may hold values from -1 to 1
Outputs:
- basis_next: float32 [64, 32768], P(None, ('leaf', 'box'))
- hessenberg: float32 [64, 64], replicated
- factor: float32 [64, 64], replicated
Inputs may be any that keep to these rules, and one draw needn't show every extreme that they name: `near_list`: entry 0 of a box's row is the box itself. Every entry lies in the box's own group of 64 consecutive boxes (groups aligned), and at most 8 boxes before the first or after the last box of the box's aligned block of 8 boxes. `far_list`: every entry lies in the box's own aligned group of 64 consecutive boxes. `coarse_list`: entries may name any parent. `krylov_block`: rows differ in scale. `points`: the panels of leaf box b lie in the cell of a regular grid of the unit cube that the Morton code b names (bit k of b counts along coordinate k mod 3).
All inputs are finite; a program needn't handle non-finite values.
Results may differ from a plain program's by a relative error of at most 0.0025.
Values sent between devices are 32-bit elements; how exact they have to be, the bound alone decides.
A program may use at most 64 MiB of HBM per device.

v0:
```python
import jax
import jax.numpy as jnp
from jax import lax
from jax.sharding import PartitionSpec as P

HIGHEST_PRECISION = lax.Precision.HIGHEST


def padded(cells, sides, width):
    for axis, dim in sides:
        count = lax.axis_size(axis)
        ends = count - 1
        head = lax.slice_in_dim(cells, 0, width, axis=dim)
        tail = lax.slice_in_dim(cells, cells.shape[dim] - width, cells.shape[dim], axis=dim)
        cells = jnp.concatenate(
            [
                lax.ppermute(tail, axis, [(i, (i + 1) % count) for i in range(ends)]),
                cells,
                lax.ppermute(head, axis, [((i + 1) % count, i) for i in range(ends)]),
            ],
            axis=dim,
        )
    return cells


def pairwise(target, source, source_values, scale_count):
    first = target[0][:, None] - source[0][None, :]
    second = target[1][:, None] - source[1][None, :]
    third = target[2][:, None] - source[2][None, :]
    squared = first * first + second * second + third * third
    green = source[4][None, :] / (
        scale_count * jnp.sqrt(squared + target[3][:, None] * source[3][None, :])
    )
    return jnp.dot(source_values, green.T, precision=HIGHEST_PRECISION)


def make_gather(wanted, shard_rows):
    slots = jnp.arange(shard_rows.shape[0], dtype=jnp.int32)
    one_hot = (wanted[:, None] == slots[None, :]).astype(jnp.float32)
    return jnp.dot(one_hot, shard_rows, precision=HIGHEST_PRECISION)


def apply_couplings(flat_table, classes, counts, selected, rank_size, column_count):
    entries = classes.shape[1]
    class_count = flat_table.shape[0]
    one_hot = (
        classes.reshape(-1)[:, None] == jnp.arange(class_count, dtype=jnp.int32)[None, :]
    ).astype(jnp.float32)
    live_mask = (
        (jnp.arange(entries, dtype=jnp.int32)[None, :] < counts[:, None])
        .astype(jnp.float32)
        .reshape(-1, 1)
    )
    matrices = jnp.dot(one_hot * live_mask, flat_table, precision=HIGHEST_PRECISION).reshape(
        -1, entries, rank_size, rank_size
    )
    chosen = selected.reshape(-1, entries, rank_size, column_count)
    return jnp.einsum("berk,bekq->brq", matrices, chosen, precision=HIGHEST_PRECISION)


def per_device(
    krylov_block,
    bases,
    points,
    panel_size,
    panel_weight,
    near_list,
    far_list,
    far_class,
    far_count,
    coarse_list,
    coarse_class,
    coarse_count,
    couple_fine,
    couple_coarse,
    up_transfer,
    down_transfer,
):
    column_count = krylov_block.shape[0]
    rank_size = bases.shape[0]
    box_count = near_list.shape[0]
    box_width = krylov_block.shape[1] // box_count
    near_count = near_list.shape[1]
    box_devices = lax.axis_size("box")
    device = lax.axis_index("leaf") * box_devices + lax.axis_index("box")
    first_box = device * box_count
    panels = krylov_block.shape[1] * lax.axis_size("leaf") * box_devices
    block_values = krylov_block.reshape(column_count, box_count, box_width)
    block_basis = bases.reshape(rank_size, box_count, box_width)
    geometry = jnp.concatenate([points, panel_size[None, :], panel_weight[None, :]], 0).reshape(
        5, box_count, box_width
    )
    stacked = jnp.concatenate([block_values, geometry], 0)
    extended = padded(stacked, (("box", 1),), box_count)

    def near_one(box_index):
        local_index = near_list[box_index] - (first_box - box_count)
        source = jnp.take(extended, local_index, axis=1).reshape(column_count + 5, -1)
        target = lax.dynamic_index_in_dim(geometry, box_index, 1, keepdims=False)
        return pairwise(
            target, source[column_count:], source[:column_count], box_width * near_count
        )

    near_field = lax.map(near_one, jnp.arange(box_count, dtype=jnp.int32))
    fine_poles = jnp.einsum("rbm,qbm->brq", block_basis, block_values, precision=HIGHEST_PRECISION)
    coarse_pole = jnp.einsum("ckr,ckq->rq", up_transfer, fine_poles, precision=HIGHEST_PRECISION)
    pole_size = rank_size * column_count
    group_first = lax.axis_index("leaf") * box_devices * box_count
    wanted = (far_list - group_first).reshape(-1)
    selected = make_gather(
        wanted, lax.all_gather(fine_poles.reshape(box_count, pole_size), "box", axis=0, tiled=True)
    )
    coarse_table = couple_coarse.reshape(couple_coarse.shape[0], -1)
    wanted_coarse = coarse_list.reshape(-1)
    selected_coarse = make_gather(
        wanted_coarse,
        lax.all_gather(coarse_pole.reshape(1, pole_size), ("leaf", "box"), axis=0, tiled=True),
    )
    coarse_local = apply_couplings(
        coarse_table, coarse_class, coarse_count, selected_coarse, rank_size, column_count
    )[0]
    fine_local = apply_couplings(
        couple_fine.reshape(couple_fine.shape[0], -1),
        far_class,
        far_count,
        selected,
        rank_size,
        column_count,
    )
    fine_local = fine_local + jnp.einsum(
        "crk,kq->crq", down_transfer, coarse_local, precision=HIGHEST_PRECISION
    )
    far_field = jnp.einsum("rcm,crq->cqm", block_basis, fine_local, precision=HIGHEST_PRECISION)
    product = (
        (far_field + near_field).transpose(1, 0, 2).reshape(column_count, box_count * box_width)
    )
    basis_gram, mixed_gram, image_gram = lax.psum(
        (
            jnp.dot(krylov_block, krylov_block.T, precision=HIGHEST_PRECISION),
            jnp.dot(krylov_block, product.T, precision=HIGHEST_PRECISION),
            jnp.dot(product, product.T, precision=HIGHEST_PRECISION),
        ),
        ("leaf", "box"),
    )
    hessenberg = mixed_gram / panels
    residual = product - jnp.dot(hessenberg.T, krylov_block, precision=HIGHEST_PRECISION)
    corrected = (
        image_gram
        - jnp.dot(mixed_gram.T, hessenberg, precision=HIGHEST_PRECISION)
        - jnp.dot(hessenberg.T, mixed_gram, precision=HIGHEST_PRECISION)
    )
    corrected = corrected + jnp.dot(
        jnp.dot(hessenberg.T, basis_gram, precision=HIGHEST_PRECISION),
        hessenberg,
        precision=HIGHEST_PRECISION,
    )
    gram_matrix = corrected / panels
    factor = jnp.linalg.cholesky(gram_matrix)
    basis_next = lax.linalg.triangular_solve(factor, residual, left_side=True, lower=True)
    return (basis_next, hessenberg, factor)


def solution(mesh):
    in_specs = (
        P(None, ("leaf", "box")),
        P(None, ("leaf", "box")),
        P(None, ("leaf", "box")),
        P(("leaf", "box")),
        P(("leaf", "box")),
        P(("leaf", "box"), None),
        P(("leaf", "box"), None),
        P(("leaf", "box"), None),
        P(("leaf", "box")),
        P(("leaf", "box"), None),
        P(("leaf", "box"), None),
        P(("leaf", "box")),
        P(),
        P(),
        P(),
        P(),
    )
    out_specs = (P(None, ("leaf", "box")), P(), P())
    return jax.shard_map(
        per_device, mesh=mesh, in_specs=in_specs, out_specs=out_specs, check_vma=False
    )
```

profile of v0, /device:TPU:0, one launch (start us, length us, event | category | flops | bytes accessed | tf_op | source)
XLA Modules:
  0.0 194.7 jit_solution(4107406261491477847)
XLA Ops:
  0.7 0.8 copy.148
  1.5 1.0 copy.108
  2.5 1.4 pad_maximum_fusion.1
  3.9 1.3 collective-permute-start.1
  5.2 3.7 %collective-permute-start = (f32[69,8,128]{2,1,0:T(8,128)}, f32[69,8,128]{2,1,0:T(8,128)}, u32[]{:S(2)}, u32[]{:S(2)}) collective-permute-start(f32[69,8,128]{2,1,0:T(8,128)} %pad_maximum_fusion.1), channel_id=1, source_target_pairs={{0,1},{1,2},{2,3},{3,4},{4,5},{5,6},{6,7},{8,9},{9,10},{10,11},{11... | collective-permute-start | bytes 847880 | tf_op jit(solution)/shard_map/ppermute | solution.py:17
  10.9 1.4 copy.78
  12.2 1.3 fusion.81
  13.5 1.1 reshape.248
  16.1 44.3 %all-gather = f32[32,1,2048]{2,1,0:T(1,128)S(1)} all-gather(f32[1,1,2048]{2,1,0:T(1,128)S(1)} %reshape.265), channel_id=1, replica_groups=mesh['leaf'=4,'box'=8] {'leaf','box'}, dimensions={0}, use_global_device_ids=true | all-gather | bytes 270336 | tf_op jit(solution)/shard_map/all_gather | solution.py:117
  60.6 0.8 reshape.255
  61.4 15.0 %all_gather.6 = f32[64,2048]{1,0:T(8,128)S(1)} all-gather(f32[8,2048]{1,0:T(8,128)S(1)} %reshape.251), channel_id=1, replica_groups=mesh['leaf'=4,'box'=8] {'box'}, dimensions={0}, use_global_device_ids=true | all-gather | bytes 589824 | tf_op jit(solution)/shard_map/all_gather | solution.py:111
  77.6 1.1 fusion.50
  78.7 1.5 fusion.48
  80.1 2.1 %fusion.46 = f32[8,12,32,32]{3,0,2,1:T(8,128)S(1)} fusion(f32[32,32,16]{1,0,2:T(8,128)S(1)} %dot_general.74, f32[8,12]{0,1:T(8,128)} %fusion.81, s32[8,12]{0,1:T(8,128)} %copy.78), kind=kOutput, calls=%fused_computation.69 | convolution fusion | flops 18877440 | bytes 459520 | tf_op jit(solution)/shard_map/dot_general | solution.py:54
  82.3 2.1 %fusion.33 = f32[8,32,64]{2,1,0:T(8,128)S(1)} fusion(f32[8,12,32,64]{3,2,1,0:T(8,128)S(1)} %reshape.252, f32[8,12,32,32]{3,0,2,1:T(8,128)S(1)} %fusion.46), kind=kOutput, calls=%fused_computation.49 | convolution fusion | flops 75497472 | bytes 1245184 | tf_op jit(solution)/shard_map/berk,bekq->brq/dot_general | solution.py:58
  85.1 1.1 pad_maximum_fusion
  86.4 52.3 %while.12 = (s32[]{:T(128)}, f32[8,64,128]{2,1,0:T(8,128)S(1)}, s32[8]{0:T(128)S(1)}, s32[8,16]{1,0:T(8,128)}, s32[]{:T(128)}, /*index=5*/f32[69,24,128]{2,0,1:T...) while((s32[]{:T(128)}, f32[8,64,128]{2,1,0:T(8,128)S(1)}, ...), condition=%wide.region_1.2_spmd, body=%wide.region_0.1_spmd.sunk | while | flops 204614832 | bytes 2951771 | solution.py:104
  89.0 0.7 compare_and_fusion.2
  91.2 1.8 fusion.126
  95.5 0.7 compare_and_fusion.2
  97.7 1.8 fusion.126
  104.2 1.8 fusion.126
  110.8 1.8 fusion.126
  117.3 1.8 fusion.126
  123.8 1.8 fusion.126
  130.4 1.8 fusion.126
  136.9 1.8 fusion.126
  140.1 38.9 %all-reduce = (f32[64,64]{0,1:T(8,128)S(1)}, f32[64,64]{0,1:T(8,128)S(1)}, f32[64,64]{1,0:T(8,128)S(1)}) all-reduce(f32[64,64]{0,1:T(8,128)S(1)} %convolution_bitcast_fusion.2, f32[64,64]{0,1:T(8,128)S(1)} %convolution_bitcast_fusion.3, f32[64,64]{1,0:T(8,128)S(1)} %fusion.94), channel_id=1, replica_groups=mesh['leaf'=4,'box'=8] {'leaf','box'}, use_global_device_ids=true, to_apply=%region_3.4 | all-reduce | flops 12288 | bytes 98304 | tf_op jit(solution)/shard_map/psum | solution.py:137
  180.9 5.8 %cholesky.16 = f32[64,64]{1,0:T(8,128)S(1)} custom-call(f32[64,64]{1,0:T(8,128)S(1)} %fusion.63), custom_call_target="Cholesky" | custom-call | tf_op jit(solution)/shard_map/jit(cholesky)/cholesky | solution.py:158
  187.4 1.3 select_bitcast_fusion.1
  188.7 4.9 %custom-call.6 = f32[1,64,64]{1,2,0:T(8,128)S(1)} custom-call(f32[1,64,64]{2,1,0:T(8,128)S(1)} %get-tuple-element.141), custom_call_target="InvertDiagBlocksLowerTriangular" | custom-call | tf_op jit(solution)/shard_map/triangular_solve | solution.py:159
  193.6 1.1 fusion.61
  (115 shorter events, 29.3 us)
Async XLA Ops:
  0.6 14.1 %copy-start = (f32[32,1024]{1,0:T(8,128)S(1)}, f32[32,1024]{1,0:T(8,128)}, u32[]{:S(2)}) copy-start(f32[32,1024]{1,0:T(8,128)} %param.19) | copy-start | bytes 393220
  0.6 14.1 %copy-start.1 = (f32[64,1024]{1,0:T(8,128)S(1)}, f32[64,1024]{1,0:T(8,128)}, u32[]{:S(2)}) copy-start(f32[64,1024]{1,0:T(8,128)} %param.18) | copy-start | bytes 786436
  0.7 13.9 %copy-start.2 = (f32[16,32,32]{2,1,0:T(8,128)S(1)}, f32[16,32,32]{2,1,0:T(8,128)}, u32[]{:S(2)}) copy-start(f32[16,32,32]{2,1,0:T(8,128)} %param.31) | copy-start | bytes 196612
  0.7 14.7 %copy-start.4 = (f32[8,32,32]{2,1,0:T(8,128)S(1)}, f32[8,32,32]{2,1,0:T(8,128)}, u32[]{:S(2)}) copy-start(f32[8,32,32]{2,1,0:T(8,128)} %param.32) | copy-start | bytes 98308
  2.5 57.9 %copy-start.7 = (s32[1,16]{1,0:T(1,128)S(1)}, s32[1,16]{1,0:T(1,128)}, u32[]{:S(2)}) copy-start(s32[1,16]{1,0:T(1,128)} %param.27) | copy-start | bytes 196
  3.9 81.2 %collective-permute-start.1 = (f32[69,8,128]{2,1,0:T(8,128)}, f32[69,8,128]{2,1,0:T(8,128)}, u32[]{:S(2)}, u32[]{:S(2)}) collective-permute-start(f32[69,8,128]{2,1,0:T(8,128)} %pad_maximum_fusion.1), channel_id=1, source_target_pairs={{1,0},{2,1},{3,2},{4,3},{5,4},{6,5},{7,6},{9,8},{10,9},{11,10},{12... | collective-permute-start | bytes 847880 | tf_op jit(solution)/shard_map/ppermute | solution.py:19
  5.2 79.9 %collective-permute-start = (f32[69,8,128]{2,1,0:T(8,128)}, f32[69,8,128]{2,1,0:T(8,128)}, u32[]{:S(2)}, u32[]{:S(2)}) collective-permute-start(f32[69,8,128]{2,1,0:T(8,128)} %pad_maximum_fusion.1), channel_id=1, source_target_pairs={{0,1},{1,2},{2,3},{3,4},{4,5},{5,6},{6,7},{8,9},{9,10},{10,11},{11... | collective-permute-start | bytes 847880 | tf_op jit(solution)/shard_map/ppermute | solution.py:17
  76.4 1.2 copy-start.8
  82.3 2.2 %copy-start.3 = (f32[8,32,32]{2,1,0:T(8,128)S(1)}, f32[8,32,32]{2,1,0:T(8,128)}, u32[]{:S(2)}) copy-start(f32[8,32,32]{2,1,0:T(8,128)} %param.33) | copy-start | bytes 98308
  82.3 2.4 %copy-start.5 = (f32[1024]{0:T(1024)S(1)}, f32[1024]{0:T(1024)}, u32[]{:S(2)}) copy-start(f32[1024]{0:T(1024)} %param.22) | copy-start | bytes 12292
  82.3 2.4 %copy-start.6 = (f32[1024]{0:T(1024)S(1)}, f32[1024]{0:T(1024)}, u32[]{:S(2)}) copy-start(f32[1024]{0:T(1024)} %param.21) | copy-start | bytes 12292
where the time goes:
time: 196 us; the launch traced here: 195 us
  blocking collectives  98.1 us (50%)
  other arithmetic  29.8 us (15%)
  matrix products  27.1 us (14%)
  local copies, waits for them, and re-layouts  17 us (9%)
  loops' own time  16 us (8%)
  starting transfers between devices  5.02 us (3%)
    all_gather x1, blocking collectives, per_device(): lax.all_gather(coarse_pole.reshape(1, pole_size), ('leaf', 'box'), axis=0...  44.3 us
    psum x1, blocking collectives, per_device(): lax.psum((jnp.dot(krylov_block, krylov_block.T, precision=HIGHEST_PRECISI...  38.9 us
    another operation x1, loops' own time, per_device(): near_field = lax.map(near_one, jnp.arange(box_count, dtype=jnp.int32))  16 us
    all_gather x1, blocking collectives, per_device(): lax.all_gather(fine_poles.reshape(box_count, pole_size), 'box', axis=0, t...  15 us
    dot_general x8, matrix products, pairwise(): return jnp.dot(source_values, green.T, precision=HIGHEST_PRECISION)  14.5 us
    another operation x3, other arithmetic, per_device(): factor = jnp.linalg.cholesky(gram_matrix)  6.52 us
    select_n x16, other arithmetic, near_one(): jnp.take(extended, local_index, axis=1).reshape(column_count + 5, -1)  6.4 us
    another operation x2, other arithmetic, per_device(): lax.linalg.triangular_solve(factor, residual, left_side=True, lower=True)  6.16 us
  transfers between devices with their start and end apart: 2, of which 0 were waited for; matrix products, arithmetic and copies ran while one was open for 8% of the time, Pallas kernels for 0%

commit v1 on v0

v1 whole, which is shorter than its diff:
```python
import functools

import jax
import jax.numpy as jnp
from jax import lax
from jax.experimental import pallas as pl
from jax.experimental.pallas import tpu as pltpu
from jax.sharding import PartitionSpec as P

HIGHEST = lax.Precision.HIGHEST
MESH = pl.DeviceIdType.MESH
F32 = jnp.float32
BF16 = jnp.bfloat16


def nn(a, b):
    return jnp.dot(a, b, precision=HIGHEST, preferred_element_type=F32)


def nt(a, b):
    return lax.dot_general(
        a, b, (((1,), (1,)), ((), ())), precision=HIGHEST, preferred_element_type=F32
    )


def split(x):
    high = x.astype(BF16)
    return high, (x - high.astype(F32)).astype(BF16)


def product_kernel(
    n_leaf, n_box, nb, width, scale,
    k_ref, b_ref, pts_ref, size_ref, weight_ref,
    near_ref, flist_ref, fclass_ref, fcount_ref, clist_ref, cclass_ref, ccount_ref,
    cf_ref, cc_ref, up_ref, down_ref,
    prod_ref, red_ref,
    ext_k, ext_g, kcat, geo_t, fbuf, cleaf, cbuf, fpole, cpole, tfine, tcoarse, dloc,
    rbuf, rrecv, lrecv, gath,
    nk_s, nk_r, ng_s, ng_r, f_s, f_r, ff_s, ff_r, c_s, c_r, cf_s, cf_r, cl_s, cl_r,
    r_s, r_r, l_s, l_r, g_s, g_r,
):
    q = k_ref.shape[0]
    r = b_ref.shape[0]
    leaf = lax.axis_index("leaf")
    box = lax.axis_index("box")
    nz = n_box // 2
    core = lax.rem(box, 2)
    z = box // 2
    sibling = 2 * z + (1 - core)
    near_count = near_ref.shape[1]
    far_count = flist_ref.shape[1]
    coarse_count = clist_ref.shape[1]
    first_box = (leaf * n_box + box) * nb
    group_first = leaf * n_box * nb

    barrier = pltpu.get_barrier_semaphore()
    for d in range(1, n_box):
        pl.semaphore_signal(
            barrier, inc=1, device_id=(leaf, lax.rem(box + d, n_box)), device_id_type=MESH
        )
    for d in range(1, n_leaf):
        pl.semaphore_signal(
            barrier, inc=1, device_id=(lax.rem(leaf + d, n_leaf), box), device_id_type=MESH
        )

    def remote(src, dst, s_sem, r_sem, dev):
        return pltpu.make_async_remote_copy(
            src_ref=src, dst_ref=dst, send_sem=s_sem, recv_sem=r_sem,
            device_id=dev, device_id_type=MESH,
        )

    weights = weight_ref[...] * (1.0 / scale)
    weighted = k_ref[...] * weights
    geo = jnp.concatenate(
        [pts_ref[...], size_ref[...], weight_ref[...], pts_ref[...]], axis=0
    )
    for b in range(nb):
        lanes = slice(b * width, (b + 1) * width)
        ext_k[nb + b] = weighted[:, lanes]
        ext_g[nb + b] = geo[:, lanes]
        geo_t[b] = geo[:, lanes].T

    pl.semaphore_wait(barrier, n_box - 1 + n_leaf - 1)

    right = (leaf, lax.rem(box + 1, n_box))
    left = (leaf, lax.rem(box + n_box - 1, n_box))
    own = pl.ds(nb, nb)
    low = pl.ds(0, nb)
    top = pl.ds(2 * nb, nb)
    k_right = remote(ext_k.at[own], ext_k.at[low], nk_s.at[0], nk_r.at[0], right)
    g_right = remote(ext_g.at[own], ext_g.at[low], ng_s.at[0], ng_r.at[0], right)
    k_left = remote(ext_k.at[own], ext_k.at[top], nk_s.at[1], nk_r.at[1], left)
    g_left = remote(ext_g.at[own], ext_g.at[top], ng_s.at[1], ng_r.at[1], left)

    @pl.when(box < n_box - 1)
    def _():
        k_right.start()
        g_right.start()

    @pl.when(box > 0)
    def _():
        k_left.start()
        g_left.start()

    @pl.when(box == 0)
    def _():
        ext_k[low] = jnp.zeros((nb, q, width), F32)
        ext_g[low] = jnp.zeros((nb, 8, width), F32)

    @pl.when(box == n_box - 1)
    def _():
        ext_k[top] = jnp.zeros((nb, q, width), F32)
        ext_g[top] = jnp.zeros((nb, 8, width), F32)

    poles = []
    for b in range(nb):
        lanes = slice(b * width, (b + 1) * width)
        poles.append(nt(b_ref[:, lanes], k_ref[:, lanes]))
    for h in range(nb // 2):
        fbuf[box, h * r : (h + 1) * r, :] = jnp.concatenate(
            [poles[2 * h], poles[2 * h + 1]], axis=1
        )

    def spread(buf, s_sems, r_sems, fs_sems, fr_sems):
        mine = buf.at[box]
        copies = [remote(mine, mine, fs_sems.at[0], fr_sems.at[0], (leaf, sibling))]
        for d in range(1, nz):
            peer = 2 * lax.rem(z + d, nz) + core
            copies.append(remote(mine, mine, s_sems.at[d], r_sems.at[d], (leaf, peer)))
        return copies

    def forward(buf, fs_sems, fr_sems):
        result = []
        for d in range(1, nz):
            source = 2 * lax.rem(z + nz - d, nz) + core
            slot = buf.at[source]
            result.append(remote(slot, slot, fs_sems.at[d], fr_sems.at[d], (leaf, sibling)))
        return result

    fine_out = spread(fbuf, f_s, f_r, ff_s, ff_r)
    for copy in fine_out:
        copy.start()

    cpole_own = nn(up_ref[...].T, jnp.concatenate(poles, axis=0))
    cleaf[leaf] = jnp.concatenate([cpole_own, cpole_own], axis=1)
    leaf_out = [
        remote(
            cleaf.at[leaf], cleaf.at[leaf], cl_s.at[d], cl_r.at[d],
            (lax.rem(leaf + d, n_leaf), box),
        )
        for d in range(1, n_leaf)
    ]
    for copy in leaf_out:
        copy.start()

    def to_split(i, carry):
        high, rest = split(ext_k[i])
        kcat[i] = jnp.concatenate([high, rest], axis=0)
        return carry

    lax.fori_loop(nb, 2 * nb, to_split, 0)
    lane4 = lax.broadcasted_iota(jnp.int32, (r, 4 * r), 1) // r
    for c in range(cf_ref.shape[0]):
        tfine[c] = jnp.concatenate([cf_ref[c]] * 4, axis=1)
    for c in range(cc_ref.shape[0]):
        tcoarse[c] = jnp.concatenate([cc_ref[c]] * 4, axis=1)

    for copy in leaf_out:
        copy.wait_recv()
    for h in range(n_leaf // 2):
        cbuf[box, h * r : (h + 1) * r, :] = jnp.concatenate(
            [cleaf[2 * h][:, :q], cleaf[2 * h + 1][:, :q]], axis=1
        )
    coarse_out = spread(cbuf, c_s, c_r, cf_s, cf_r)
    for copy in coarse_out:
        copy.start()

    @pl.when(box > 0)
    def _():
        k_right.wait_recv()
        g_right.wait_recv()

    @pl.when(box < n_box - 1)
    def _():
        k_left.wait_recv()
        g_left.wait_recv()

    lax.fori_loop(0, nb, to_split, 0)
    lax.fori_loop(2 * nb, 3 * nb, to_split, 0)

    shift = nb - first_box

    def near_box(b, carry):
        target = geo_t[b]
        columns = [jnp.broadcast_to(target[:, c : c + 1], (width, width)) for c in range(4)]

        def pair(t, total):
            greens = []
            sources = []
            for side in range(2):
                i = jnp.clip(near_ref[b, 2 * t + side] + shift, 0, 3 * nb - 1)
                g = ext_g[i]
                first = columns[0] - g[0:1]
                second = columns[1] - g[1:2]
                third = columns[2] - g[2:3]
                squared = first * first + second * second + third * third
                greens.append(lax.rsqrt(squared + columns[3] * g[3:4]))
                sources.append(kcat[i])
            high, rest = split(jnp.concatenate(greens, axis=1))
            both = jnp.concatenate([high, rest], axis=0)
            source = jnp.concatenate(sources, axis=1)
            return total + lax.dot_general(
                source, both, (((1,), (1,)), ((), ())), preferred_element_type=F32
            )

        total = lax.fori_loop(
            0, near_count // 2, pair, jnp.zeros((2 * q, 2 * width), F32)
        )
        half = total[:, :width] + total[:, width:]
        prod_ref[:, pl.ds(pl.multiple_of(b * width, width), width)] = half[:q] + half[q:]
        return carry

    def near_range(lo, hi):
        lax.fori_loop(lo, hi, near_box, 0)

    near_range(0, nb // 2)
    fine_fwd = forward(fbuf, ff_s, ff_r)
    for d in range(1, nz):
        fine_out[d].wait_recv()
        fine_fwd[d - 1].start()
    coarse_fwd = forward(cbuf, cf_s, cf_r)
    for d in range(1, nz):
        coarse_out[d].wait_recv()
        coarse_fwd[d - 1].start()
    near_range(nb // 2, nb)

    for copy in [coarse_out[0]] + coarse_fwd + [fine_out[0]] + fine_fwd:
        copy.wait_recv()

    def open_coarse(i, carry):
        for h in range(n_leaf // 2):
            rows = cbuf[i, h * r : (h + 1) * r, :]
            cpole[2 * h * n_box + i] = rows[:, :q]
            cpole[(2 * h + 1) * n_box + i] = rows[:, q:]
        return carry

    lax.fori_loop(0, n_box, open_coarse, 0)

    def open_fine(i, carry):
        for h in range(nb // 2):
            rows = fbuf[i, h * r : (h + 1) * r, :]
            fpole[i * nb + 2 * h] = rows[:, :q]
            fpole[i * nb + 2 * h + 1] = rows[:, q:]
        return carry

    lax.fori_loop(0, n_box, open_fine, 0)

    def coupled(table, class_of, pole, index_of, live, entries):
        left_side = []
        for group in range(entries // 4):
            block = None
            for side in range(4):
                e = 4 * group + side
                mask = jnp.where(e < live, 1.0, 0.0).astype(F32)
                piece = table[class_of(e)] * mask
                block = piece if side == 0 else jnp.where(lane4 == side, piece, block)
            left_side.append(block)
        right_side = [pole[index_of(e)] for e in range(entries)]
        return nn(jnp.concatenate(left_side, axis=1), jnp.concatenate(right_side, axis=0))

    coarse_local = coupled(
        tcoarse, lambda e: cclass_ref[0, e], cpole, lambda e: clist_ref[0, e],
        ccount_ref[0], coarse_count,
    )
    lowered = nn(down_ref[...], coarse_local)
    for b in range(nb):
        dloc[b] = lowered[b * r : (b + 1) * r]

    def far_box(b, carry):
        local = dloc[b] + coupled(
            tfine, lambda e: fclass_ref[b, e], fpole,
            lambda e: jnp.clip(flist_ref[b, e] - group_first, 0, n_box * nb - 1),
            fcount_ref[b], far_count,
        )
        lanes = pl.ds(pl.multiple_of(b * width, width), width)
        prod_ref[:, lanes] = prod_ref[:, lanes] + nn(local.T, b_ref[:, lanes])
        return carry

    lax.fori_loop(0, nb, far_box, 0)

    stacked = jnp.concatenate([k_ref[...], prod_ref[...]], axis=0)
    gram = nt(stacked, stacked)
    share = rbuf.shape[1]
    for s in range(n_box):
        rbuf[s] = gram[s * share : (s + 1) * share]
    r_out = []
    for d in range(1, n_box):
        peer = lax.rem(box + d, n_box)
        r_out.append(
            remote(rbuf.at[peer], rrecv.at[box], r_s.at[d], r_r.at[d], (leaf, peer))
        )
        r_out[-1].start()
    rrecv[box] = rbuf[box]
    for copy in r_out:
        copy.wait_recv()
    part = rrecv[0]
    for s in range(1, n_box):
        part = part + rrecv[s]
    lrecv[leaf] = part
    l_out = []
    for d in range(1, n_leaf):
        peer = lax.rem(leaf + d, n_leaf)
        l_out.append(
            remote(lrecv.at[leaf], lrecv.at[leaf], l_s.at[d], l_r.at[d], (peer, box))
        )
        l_out[-1].start()
    for copy in l_out:
        copy.wait_recv()
    part = lrecv[0]
    for s in range(1, n_leaf):
        part = part + lrecv[s]
    gath[box] = part
    g_out = []
    for d in range(1, n_box):
        peer = lax.rem(box + d, n_box)
        g_out.append(remote(gath.at[box], gath.at[box], g_s.at[d], g_r.at[d], (leaf, peer)))
        g_out[-1].start()
    for copy in g_out:
        copy.wait_recv()
    red_ref[...] = gath[...]

    @pl.when(box < n_box - 1)
    def _():
        k_right.wait_send()
        g_right.wait_send()

    @pl.when(box > 0)
    def _():
        k_left.wait_send()
        g_left.wait_send()

    for copy in fine_out + fine_fwd + leaf_out + coarse_out + coarse_fwd + r_out + l_out + g_out:
        copy.wait_send()


def finish_kernel(panels, k_ref, prod_ref, red_ref, basis_ref, hess_ref, factor_ref):
    q = k_ref.shape[0]
    red = red_ref[...]
    basis_gram = red[:q, :q]
    mixed = red[:q, q:]
    mixed_t = red[q:, :q]
    image = red[q:, q:]
    inverse = 1.0 / panels
    hess = mixed * inverse
    hess_t = mixed_t * inverse
    hess_ref[...] = hess
    corrected = image - nn(mixed_t, hess) - nn(hess_t, mixed)
    corrected = (corrected + nn(nn(hess_t, basis_gram), hess)) * inverse
    eye = (
        lax.broadcasted_iota(jnp.int32, (q, q), 0) == lax.broadcasted_iota(jnp.int32, (q, q), 1)
    ).astype(F32)
    start = jnp.concatenate([corrected, eye], axis=1)
    tiles = [start[8 * t : 8 * t + 8] for t in range(q // 8)]
    row_id = lax.broadcasted_iota(jnp.int32, (8, 2 * q), 0)
    for p in range(q // 8):
        cols = [
            [jnp.broadcast_to(tiles[t][:, 8 * p + c : 8 * p + c + 1], (8, 2 * q)) for t in range(p, q // 8)]
            for c in range(8)
        ]
        for c in range(8):
            pivot = cols[c][0][c : c + 1]
            scale = lax.rsqrt(pivot)
            row = tiles[p][c : c + 1] * scale
            scaled = [tile * scale for tile in cols[c]]
            scaled[0] = jnp.where(row_id > c, scaled[0], 0.0)
            for j in range(c + 1, 8):
                value = cols[j][0][c : c + 1] * scale
                cols[j] = [x - s * value for x, s in zip(cols[j], scaled)]
            tiles[p] = jnp.where(row_id == c, row, tiles[p] - scaled[0] * row)
            for t in range(p + 1, q // 8):
                tiles[t] = tiles[t] - scaled[t - p] * row
    done = jnp.concatenate(tiles, axis=0)
    lower = done[:, :q].T
    keep = lax.broadcasted_iota(jnp.int32, (q, q), 0) >= lax.broadcasted_iota(jnp.int32, (q, q), 1)
    factor_ref[...] = jnp.where(keep, lower, 0.0)
    solve = jnp.where(keep, done[:, q:], 0.0)
    residual = prod_ref[...] - nn(hess_t, k_ref[...])
    basis_ref[...] = nn(solve, residual)


def per_device(
    krylov_block, bases, points, panel_size, panel_weight, near_list, far_list, far_class,
    far_count, coarse_list, coarse_class, coarse_count, couple_fine, couple_coarse,
    up_transfer, down_transfer,
):
    q, local = krylov_block.shape
    r = bases.shape[0]
    nb = near_list.shape[0]
    width = local // nb
    n_leaf = lax.axis_size("leaf")
    n_box = lax.axis_size("box")
    nz = n_box // 2
    share = 2 * q // n_box
    panels = local * n_leaf * n_box
    vmem = pl.BlockSpec(memory_space=pltpu.VMEM)
    smem = pl.BlockSpec(memory_space=pltpu.SMEM)
    dma = lambda n: pltpu.SemaphoreType.DMA((n,))
    product, reduced = pl.pallas_call(
        functools.partial(
            product_kernel, n_leaf, n_box, nb, width, float(width * near_list.shape[1])
        ),
        out_shape=(
            jax.ShapeDtypeStruct((q, local), F32),
            jax.ShapeDtypeStruct((n_box, share, 2 * q), F32),
        ),
        in_specs=[vmem] * 5 + [smem] * 7 + [vmem] * 4,
        out_specs=(vmem, vmem),
        scratch_shapes=[
            pltpu.VMEM((3 * nb, q, width), F32),
            pltpu.VMEM((3 * nb, 8, width), F32),
            pltpu.VMEM((3 * nb, 2 * q, width), BF16),
            pltpu.VMEM((nb, width, 8), F32),
            pltpu.VMEM((n_box, nb // 2 * r, 2 * q), F32),
            pltpu.VMEM((n_leaf, r, 2 * q), F32),
            pltpu.VMEM((n_box, n_leaf // 2 * r, 2 * q), F32),
            pltpu.VMEM((n_box * nb, r, q), F32),
            pltpu.VMEM((n_box * n_leaf, r, q), F32),
            pltpu.VMEM((couple_fine.shape[0], r, 4 * r), F32),
            pltpu.VMEM((couple_coarse.shape[0], r, 4 * r), F32),
            pltpu.VMEM((nb, r, q), F32),
            pltpu.VMEM((n_box, share, 2 * q), F32),
            pltpu.VMEM((n_box, share, 2 * q), F32),
            pltpu.VMEM((n_leaf, share, 2 * q), F32),
            pltpu.VMEM((n_box, share, 2 * q), F32),
            dma(2), dma(2), dma(2), dma(2),
            dma(nz), dma(nz), dma(nz), dma(nz),
            dma(nz), dma(nz), dma(nz), dma(nz),
            dma(n_leaf), dma(n_leaf),
            dma(n_box), dma(n_box), dma(n_leaf), dma(n_leaf), dma(n_box), dma(n_box),
        ],
        compiler_params=pltpu.CompilerParams(
            collective_id=0, has_side_effects=True, vmem_limit_bytes=48 * 2**20
        ),
    )(
        krylov_block, bases, points, panel_size[None, :], panel_weight[None, :],
        near_list, far_list, far_class, far_count, coarse_list, coarse_class, coarse_count,
        couple_fine, couple_coarse,
        up_transfer.reshape(-1, r), down_transfer.reshape(-1, r),
    )
    return pl.pallas_call(
        functools.partial(finish_kernel, float(panels)),
        out_shape=(
            jax.ShapeDtypeStruct((q, local), F32),
            jax.ShapeDtypeStruct((q, q), F32),
            jax.ShapeDtypeStruct((q, q), F32),
        ),
        in_specs=[vmem] * 3,
        out_specs=(vmem, vmem, vmem),
        compiler_params=pltpu.CompilerParams(vmem_limit_bytes=32 * 2**20),
    )(krylov_block, product, reduced.reshape(2 * q, 2 * q))


def solution(mesh):
    split_last = P(None, ("leaf", "box"))
    split_first = P(("leaf", "box"), None)
    flat = P(("leaf", "box"))
    in_specs = (
        split_last, split_last, split_last, flat, flat,
        split_first, split_first, split_first, flat,
        split_first, split_first, flat,
        P(), P(), P(), P(),
    )
    return jax.shard_map(
        per_device, mesh=mesh, in_specs=in_specs, out_specs=(split_last, P(), P()),
        check_vma=False,
    )
```

time: 196 us -> 66.1 us (0.34)
  blocking collectives: 98.1 us -> 0 us
  Pallas kernels: 0 us -> 54.6 us
  other arithmetic: 29.8 us -> 0 us
  matrix products: 27.1 us -> 0 us
  loops' own time: 16 us -> 0 us
  local copies, waits for them, and re-layouts: 17 us -> 9.65 us
  starting transfers between devices: 5.02 us -> 0 us
    all_gather x2 -> x0, blocking collectives: 59.2 us -> none  [the longest x1 44.3 us: per_device(): lax.all_gather(coarse_pole.reshape(1, pole_size), ('leaf', 'box'), axis=0...]
    pallas_call x0 -> x2, Pallas kernels: none -> 54.6 us  [the longest x1 51.2 us: per_device(): pl.pallas_call(functools.partial(product_kernel, n_leaf, n_box, nb, width...]
    psum x1 -> x0, blocking collectives: 38.9 us -> none  [per_device(): lax.psum((jnp.dot(krylov_block, krylov_block.T, precision=HIGHEST_PRECISI...]
    dot_general x26 -> x0, matrix products: 26 us -> none  [the longest x8 14.5 us: pairwise(): return jnp.dot(source_values, green.T, precision=HIGHEST_PRECISION)]
    another operation x1 -> x0, loops' own time: 16 us -> none  [per_device(): near_field = lax.map(near_one, jnp.arange(box_count, dtype=jnp.int32))]
    another operation x5 -> x0, other arithmetic: 12.7 us -> none  [the longest x3 6.52 us: per_device(): factor = jnp.linalg.cholesky(gram_matrix)]
    select_n x16 -> x0, other arithmetic: 6.4 us -> none  [near_one(): jnp.take(extended, local_index, axis=1).reshape(column_count + 5, -1)]
    unnamed x23 -> x30, local copies, waits for them, and re-layouts: 3.99 us -> 9.65 us
  transfers between devices with their start and end apart: 2 -> 0, of which waited for: 0 -> 0; matrix products, arithmetic and copies ran while one was open for 8% -> 0% of each run, Pallas kernels for 0% -> 0%
where the time goes in v1:
time: 66.1 us; the launch traced here: 65.6 us
  Pallas kernels  54.6 us (83%)
  local copies, waits for them, and re-layouts  9.65 us (15%)
  between operations  1.36 us (2%)
    pallas_call x1, Pallas kernels, per_device(): pl.pallas_call(functools.partial(product_kernel, n_leaf, n_box, nb, width...  51.2 us
    unnamed x30, local copies, waits for them, and re-layouts  9.65 us
    pallas_call x1, Pallas kernels, per_device(): pl.pallas_call(functools.partial(finish_kernel, float(panels)), out_shape...  3.38 us

profile of v1, /device:TPU:0, one launch (start us, length us, event | category | flops | bytes accessed | tf_op | source)
XLA Modules:
  0.0 65.6 jit_solution(9470404915077456355)
XLA Ops:
  0.6 0.0 copy-start.8
  1.3 0.0 copy-start.7
  1.3 0.0 copy-start.12
  1.3 0.0 copy-start.13
  1.3 0.0 copy-done.8
  1.3 0.6 copy-done.7
  2.0 0.0 copy-done.12
  2.0 0.0 copy-done.13
  2.0 0.0 copy-start
  2.0 0.9 %copy-done = f32[64,1024]{1,0:T(8,128)S(1)} copy-done((f32[64,1024]{1,0:T(8,128)S(1)}, f32[64,1024]{1,0:T(8,128)}, u32[]{:S(2)}) %copy-start) | copy-done | bytes 262168
  3.0 0.0 copy-start.1
  3.0 0.9 %copy-done.1 = f32[16,32,32]{2,1,0:T(8,128)S(1)} copy-done((f32[16,32,32]{2,1,0:T(8,128)S(1)}, f32[16,32,32]{2,1,0:T(8,128)}, u32[]{:S(2)}) %copy-start.1) | copy-done | bytes 65560
  3.9 0.0 copy-start.2
  3.9 0.9 %copy-done.2 = f32[16,32,32]{2,1,0:T(8,128)S(1)} copy-done((f32[16,32,32]{2,1,0:T(8,128)S(1)}, f32[16,32,32]{2,1,0:T(8,128)}, u32[]{:S(2)}) %copy-start.2) | copy-done | bytes 65560
  4.9 0.0 copy-start.3
  4.9 0.9 %copy-done.3 = f32[32,1024]{1,0:T(8,128)S(1)} copy-done((f32[32,1024]{1,0:T(8,128)S(1)}, f32[32,1024]{1,0:T(8,128)}, u32[]{:S(2)}) %copy-start.3) | copy-done | bytes 131096
  5.8 0.0 copy-start.4
  5.8 0.9 %copy-done.4 = f32[8,32,32]{2,1,0:T(8,128)S(1)} copy-done((f32[8,32,32]{2,1,0:T(8,128)S(1)}, f32[8,32,32]{2,1,0:T(8,128)}, u32[]{:S(2)}) %copy-start.4) | copy-done | bytes 32792
  6.7 0.0 copy-start.5
  6.7 0.9 %copy-done.5 = f32[8,32,32]{2,1,0:T(8,128)S(1)} copy-done((f32[8,32,32]{2,1,0:T(8,128)S(1)}, f32[8,32,32]{2,1,0:T(8,128)}, u32[]{:S(2)}) %copy-start.5) | copy-done | bytes 32792
  7.6 0.0 copy-start.6
  7.6 0.7 %copy-done.6 = f32[3,1024]{1,0:T(4,128)S(1)} copy-done((f32[3,1024]{1,0:T(4,128)S(1)}, f32[3,1024]{1,0:T(4,128)}, u32[]{:S(2)}) %copy-start.6) | copy-done | bytes 12312
  8.3 0.0 copy-start.9
  8.3 0.7 %copy-done.9 = s32[8,16]{1,0:T(8,128)S(1)} copy-done((s32[8,16]{1,0:T(8,128)S(1)}, s32[8,16]{1,0:T(8,128)}, u32[]{:S(2)}) %copy-start.9) | copy-done | bytes 536
  9.0 0.0 copy-start.10
  9.0 0.7 %copy-done.10 = s32[8,12]{1,0:T(8,128)S(1)} copy-done((s32[8,12]{1,0:T(8,128)S(1)}, s32[8,12]{1,0:T(8,128)}, u32[]{:S(2)}) %copy-start.10) | copy-done | bytes 408
  9.7 0.0 copy-start.11
  9.7 0.7 %copy-done.11 = s32[8,12]{1,0:T(8,128)S(1)} copy-done((s32[8,12]{1,0:T(8,128)S(1)}, s32[8,12]{1,0:T(8,128)}, u32[]{:S(2)}) %copy-start.11) | copy-done | bytes 408
  10.3 0.0 copy-start.14
  10.3 0.7 copy-done.14
  11.0 51.2 %shard_map.175 = (f32[64,1024]{1,0:T(8,128)S(1)}, f32[8,16,128]{2,1,0:T(8,128)S(1)}) custom-call(f32[64,1024]{1,0:T(8,128)S(1)} %copy-done, f32[32,1024]{1,0:T(8,128)S(1)} %copy-done.3, f32[3,1024]{1,0:T(4,128)S(1)} %copy-done.6, f32[1,1024]{1,0:T(1,128)S(1)} %bitcast.8, f32[1,1024]{1,0:T(1,128)S(1)} %bitcast.9, s32[8,16]{1,0:T(8,128)S(1)} %copy-done.9, ...), custom_call_target="tpu_custom_call" | custom-call | tf_op jit(solution)/shard_map/pallas_call | solution.py:408
  62.2 3.4 %shard_map.176 = (f32[64,1024]{1,0:T(8,128)}, f32[64,64]{1,0:T(8,128)}, f32[64,64]{1,0:T(8,128)}) custom-call(f32[64,1024]{1,0:T(8,128)S(1)} %copy-done, f32[64,1024]{1,0:T(8,128)S(1)} %get-tuple-element.5.prod_ref, f32[128,128]{1,0:T(8,128)S(1)} %bitcast.7), custom_call_target="tpu_custom_call" | custom-call | tf_op jit(solution)/shard_map/pallas_call | solution.py:450
Async XLA Ops:
  0.6 0.7 %copy-start.8 = (f32[1024]{0:T(1024)S(1)}, f32[1024]{0:T(1024)}, u32[]{:S(2)}) copy-start(f32[1024]{0:T(1024)} %param.20) | copy-start | bytes 12292
  1.3 0.7 %copy-start.7 = (f32[1024]{0:T(1024)S(1)}, f32[1024]{0:T(1024)}, u32[]{:S(2)}) copy-start(f32[1024]{0:T(1024)} %param.19) | copy-start | bytes 12292
  1.3 0.7 %copy-start.12 = (s32[8]{0:T(128)S(1)}, s32[8]{0:T(128)}, u32[]{:S(2)}) copy-start(s32[8]{0:T(128)} %fcount_ref.1) | copy-start | bytes 100
  1.3 0.7 %copy-start.13 = (s32[1,16]{1,0:T(1,128)S(1)}, s32[1,16]{1,0:T(1,128)}, u32[]{:S(2)}) copy-start(s32[1,16]{1,0:T(1,128)} %clist_ref.1) | copy-start | bytes 196
  2.0 1.0 %copy-start = (f32[64,1024]{1,0:T(8,128)S(1)}, f32[64,1024]{1,0:T(8,128)}, u32[]{:S(2)}) copy-start(f32[64,1024]{1,0:T(8,128)} %k_ref.3) | copy-start | bytes 786436
  3.0 0.9 %copy-start.1 = (f32[16,32,32]{2,1,0:T(8,128)S(1)}, f32[16,32,32]{2,1,0:T(8,128)}, u32[]{:S(2)}) copy-start(f32[16,32,32]{2,1,0:T(8,128)} %cf_ref.1) | copy-start | bytes 196612
  3.9 0.9 %copy-start.2 = (f32[16,32,32]{2,1,0:T(8,128)S(1)}, f32[16,32,32]{2,1,0:T(8,128)}, u32[]{:S(2)}) copy-start(f32[16,32,32]{2,1,0:T(8,128)} %cc_ref.1) | copy-start | bytes 196612
  4.9 0.9 %copy-start.3 = (f32[32,1024]{1,0:T(8,128)S(1)}, f32[32,1024]{1,0:T(8,128)}, u32[]{:S(2)}) copy-start(f32[32,1024]{1,0:T(8,128)} %b_ref.1) | copy-start | bytes 393220
  5.8 0.9 %copy-start.4 = (f32[8,32,32]{2,1,0:T(8,128)S(1)}, f32[8,32,32]{2,1,0:T(8,128)}, u32[]{:S(2)}) copy-start(f32[8,32,32]{2,1,0:T(8,128)} %param.30) | copy-start | bytes 98308
  6.7 0.9 %copy-start.5 = (f32[8,32,32]{2,1,0:T(8,128)S(1)}, f32[8,32,32]{2,1,0:T(8,128)}, u32[]{:S(2)}) copy-start(f32[8,32,32]{2,1,0:T(8,128)} %param.31) | copy-start | bytes 98308
  7.6 0.7 %copy-start.6 = (f32[3,1024]{1,0:T(4,128)S(1)}, f32[3,1024]{1,0:T(4,128)}, u32[]{:S(2)}) copy-start(f32[3,1024]{1,0:T(4,128)} %pts_ref.1) | copy-start | bytes 36868
  8.3 0.7 %copy-start.9 = (s32[8,16]{1,0:T(8,128)S(1)}, s32[8,16]{1,0:T(8,128)}, u32[]{:S(2)}) copy-start(s32[8,16]{1,0:T(8,128)} %near_ref.1) | copy-start | bytes 1540
  9.0 0.7 %copy-start.10 = (s32[8,12]{1,0:T(8,128)S(1)}, s32[8,12]{1,0:T(8,128)}, u32[]{:S(2)}) copy-start(s32[8,12]{1,0:T(8,128)} %flist_ref.1) | copy-start | bytes 1156
  9.7 0.7 %copy-start.11 = (s32[8,12]{1,0:T(8,128)S(1)}, s32[8,12]{1,0:T(8,128)}, u32[]{:S(2)}) copy-start(s32[8,12]{1,0:T(8,128)} %fclass_ref.1) | copy-start | bytes 1156
  10.3 0.7 copy-start.14

commit v2 on v1

--- a/solution.py
+++ b/solution.py
@@ -34,9 +34,9 @@
     near_ref, flist_ref, fclass_ref, fcount_ref, clist_ref, cclass_ref, ccount_ref,
     cf_ref, cc_ref, up_ref, down_ref,
     prod_ref, red_ref,
-    ext_k, ext_g, kcat, geo_t, fbuf, cleaf, cbuf, fpole, cpole, tfine, tcoarse, dloc,
+    ext_k, ext_g, kcat, geo_t, greens, fbuf, lbuf, fpole, cpole, tfine, tcoarse, dloc,
     rbuf, rrecv, lrecv, gath,
-    nk_s, nk_r, ng_s, ng_r, f_s, f_r, ff_s, ff_r, c_s, c_r, cf_s, cf_r, cl_s, cl_r,
+    nk_s, nk_r, ng_s, ng_r, f_s, f_r, ff_s, ff_r, cl_s, cl_r,
     r_s, r_r, l_s, l_r, g_s, g_r,
 ):
     q = k_ref.shape[0]
@@ -94,13 +94,13 @@
 
     @pl.when(box < n_box - 1)
     def _():
+        g_right.start()
         k_right.start()
-        g_right.start()
 
     @pl.when(box > 0)
     def _():
+        g_left.start()
         k_left.start()
-        g_left.start()
 
     @pl.when(box == 0)
     def _():
@@ -121,6 +121,12 @@
             [poles[2 * h], poles[2 * h + 1]], axis=1
         )
 
+    cpole_own = nn(up_ref[...].T, jnp.concatenate(poles, axis=0))
+    fine_rows = nb // 2 * r
+    fbuf[box, fine_rows : fine_rows + r // 2, :] = jnp.concatenate(
+        [cpole_own[: r // 2], cpole_own[r // 2 :]], axis=1
+    )
+
     def spread(buf, s_sems, r_sems, fs_sems, fr_sems):
         mine = buf.at[box]
         copies = [remote(mine, mine, fs_sems.at[0], fr_sems.at[0], (leaf, sibling))]
@@ -141,18 +147,6 @@
     for copy in fine_out:
         copy.start()
 
-    cpole_own = nn(up_ref[...].T, jnp.concatenate(poles, axis=0))
-    cleaf[leaf] = jnp.concatenate([cpole_own, cpole_own], axis=1)
-    leaf_out = [
-        remote(
-            cleaf.at[leaf], cleaf.at[leaf], cl_s.at[d], cl_r.at[d],
-            (lax.rem(leaf + d, n_leaf), box),
-        )
-        for d in range(1, n_leaf)
-    ]
-    for copy in leaf_out:
-        copy.start()
-
     def to_split(i, carry):
         high, rest = split(ext_k[i])
         kcat[i] = jnp.concatenate([high, rest], axis=0)
@@ -165,86 +159,87 @@
     for c in range(cc_ref.shape[0]):
         tcoarse[c] = jnp.concatenate([cc_ref[c]] * 4, axis=1)
 
-    for copy in leaf_out:
-        copy.wait_recv()
-    for h in range(n_leaf // 2):
-        cbuf[box, h * r : (h + 1) * r, :] = jnp.concatenate(
-            [cleaf[2 * h][:, :q], cleaf[2 * h + 1][:, :q]], axis=1
-        )
-    coarse_out = spread(cbuf, c_s, c_r, cf_s, cf_r)
-    for copy in coarse_out:
-        copy.start()
-
     @pl.when(box > 0)
     def _():
-        k_right.wait_recv()
         g_right.wait_recv()
 
     @pl.when(box < n_box - 1)
     def _():
-        k_left.wait_recv()
         g_left.wait_recv()
 
-    lax.fori_loop(0, nb, to_split, 0)
-    lax.fori_loop(2 * nb, 3 * nb, to_split, 0)
-
     shift = nb - first_box
 
-    def near_box(b, carry):
+    def source_box(b, e):
+        return jnp.clip(near_ref[b, e] + shift, 0, 3 * nb - 1)
+
+    pairs = near_count // 2
+
+    def green_box(b, carry):
         target = geo_t[b]
         columns = [jnp.broadcast_to(target[:, c : c + 1], (width, width)) for c in range(4)]
 
-        def pair(t, total):
-            greens = []
-            sources = []
+        def pair(t, carry):
             for side in range(2):
-                i = jnp.clip(near_ref[b, 2 * t + side] + shift, 0, 3 * nb - 1)
-                g = ext_g[i]
+                g = ext_g[source_box(b, 2 * t + side)]
                 first = columns[0] - g[0:1]
                 second = columns[1] - g[1:2]
                 third = columns[2] - g[2:3]
                 squared = first * first + second * second + third * third
-                greens.append(lax.rsqrt(squared + columns[3] * g[3:4]))
-                sources.append(kcat[i])
-            high, rest = split(jnp.concatenate(greens, axis=1))
-            both = jnp.concatenate([high, rest], axis=0)
-            source = jnp.concatenate(sources, axis=1)
-            return total + lax.dot_general(
-                source, both, (((1,), (1,)), ((), ())), preferred_element_type=F32
+                high, rest = split(lax.rsqrt(squared + columns[3] * g[3:4]))
+                lanes = slice(side * width, (side + 1) * width)
+                greens[b * pairs + t, :width, lanes] = high
+                greens[b * pairs + t, width:, lanes] = rest
+            return carry
+
+        return lax.fori_loop(0, pairs, pair, carry)
+
+    def near_box(b, carry):
+        total = jnp.zeros((2 * q, 2 * width), F32)
+        for t in range(pairs):
+            source = jnp.concatenate(
+                [kcat[source_box(b, 2 * t)], kcat[source_box(b, 2 * t + 1)]], axis=1
             )
-
-        total = lax.fori_loop(
-            0, near_count // 2, pair, jnp.zeros((2 * q, 2 * width), F32)
-        )
+            total = total + lax.dot_general(
+                source, greens[b * pairs + t], (((1,), (1,)), ((), ())),
+                preferred_element_type=F32,
+            )
         half = total[:, :width] + total[:, width:]
         prod_ref[:, pl.ds(pl.multiple_of(b * width, width), width)] = half[:q] + half[q:]
         return carry
 
-    def near_range(lo, hi):
-        lax.fori_loop(lo, hi, near_box, 0)
-
-    near_range(0, nb // 2)
     fine_fwd = forward(fbuf, ff_s, ff_r)
+    cuts = [nb * d // nz for d in range(nz + 1)]
+    lax.fori_loop(0, cuts[1], green_box, 0)
     for d in range(1, nz):
         fine_out[d].wait_recv()
         fine_fwd[d - 1].start()
-    coarse_fwd = forward(cbuf, cf_s, cf_r)
-    for d in range(1, nz):
-        coarse_out[d].wait_recv()
-        coarse_fwd[d - 1].start()
-    near_range(nb // 2, nb)
-
-    for copy in [coarse_out[0]] + coarse_fwd + [fine_out[0]] + fine_fwd:
+        if cuts[d + 1] > cuts[d]:
+            lax.fori_loop(cuts[d], cuts[d + 1], green_box, 0)
+    for copy in [fine_out[0]] + fine_fwd:
         copy.wait_recv()
-
-    def open_coarse(i, carry):
-        for h in range(n_leaf // 2):
-            rows = cbuf[i, h * r : (h + 1) * r, :]
-            cpole[2 * h * n_box + i] = rows[:, :q]
-            cpole[(2 * h + 1) * n_box + i] = rows[:, q:]
-        return carry
-
-    lax.fori_loop(0, n_box, open_coarse, 0)
+    for i in range(n_box):
+        lbuf[leaf, i] = fbuf[i, fine_rows : fine_rows + r // 2, :]
+    leaf_out = [
+        remote(
+            lbuf.at[leaf], lbuf.at[leaf], cl_s.at[d], cl_r.at[d],
+            (lax.rem(leaf + d, n_leaf), box),
+        )
+        for d in range(1, n_leaf)
+    ]
+    for copy in leaf_out:
+        copy.start()
+
+    @pl.when(box > 0)
+    def _():
+        k_right.wait_recv()
+
+    @pl.when(box < n_box - 1)
+    def _():
+        k_left.wait_recv()
+
+    lax.fori_loop(0, nb, to_split, 0)
+    lax.fori_loop(2 * nb, 3 * nb, to_split, 0)
+    lax.fori_loop(0, nb, near_box, 0)
 
     def open_fine(i, carry):
         for h in range(nb // 2):
@@ -254,6 +249,16 @@
         return carry
 
     lax.fori_loop(0, n_box, open_fine, 0)
+
+    def open_coarse(i, carry):
+        for h in range(n_leaf):
+            rows = lbuf[h, i]
+            cpole[h * n_box + i] = jnp.concatenate([rows[:, :q], rows[:, q:]], axis=0)
+        return carry
+
+    for copy in leaf_out:
+        copy.wait_recv()
+    lax.fori_loop(0, n_box, open_coarse, 0)
 
     def coupled(table, class_of, pole, index_of, live, entries):
         left_side = []
@@ -339,7 +344,7 @@
         k_left.wait_send()
         g_left.wait_send()
 
-    for copy in fine_out + fine_fwd + leaf_out + coarse_out + coarse_fwd + r_out + l_out + g_out:
+    for copy in fine_out + fine_fwd + leaf_out + r_out + l_out + g_out:
         copy.wait_send()
 
 
@@ -420,9 +425,9 @@
             pltpu.VMEM((3 * nb, 8, width), F32),
             pltpu.VMEM((3 * nb, 2 * q, width), BF16),
             pltpu.VMEM((nb, width, 8), F32),
-            pltpu.VMEM((n_box, nb // 2 * r, 2 * q), F32),
-            pltpu.VMEM((n_leaf, r, 2 * q), F32),
-            pltpu.VMEM((n_box, n_leaf // 2 * r, 2 * q), F32),
+            pltpu.VMEM((nb * (near_list.shape[1] // 2), 2 * width, 2 * width), BF16),
+            pltpu.VMEM((n_box, nb // 2 * r + r // 2, 2 * q), F32),
+            pltpu.VMEM((n_leaf, n_box, r // 2, 2 * q), F32),
             pltpu.VMEM((n_box * nb, r, q), F32),
             pltpu.VMEM((n_box * n_leaf, r, q), F32),
             pltpu.VMEM((couple_fine.shape[0], r, 4 * r), F32),
@@ -434,12 +439,11 @@
             pltpu.VMEM((n_box, share, 2 * q), F32),
             dma(2), dma(2), dma(2), dma(2),
             dma(nz), dma(nz), dma(nz), dma(nz),
-            dma(nz), dma(nz), dma(nz), dma(nz),
             dma(n_leaf), dma(n_leaf),
             dma(n_box), dma(n_box), dma(n_leaf), dma(n_leaf), dma(n_box), dma(n_box),
         ],
         compiler_params=pltpu.CompilerParams(
-            collective_id=0, has_side_effects=True, vmem_limit_bytes=48 * 2**20
+            collective_id=0, has_side_effects=True, vmem_limit_bytes=63 * 2**20
         ),
     )(
         krylov_block, bases, points, panel_size[None, :], panel_weight[None, :],
@@ -456,7 +460,7 @@
         ),
         in_specs=[vmem] * 3,
         out_specs=(vmem, vmem, vmem),
-        compiler_params=pltpu.CompilerParams(vmem_limit_bytes=32 * 2**20),
+        compiler_params=pltpu.CompilerParams(vmem_limit_bytes=63 * 2**20),
     )(krylov_block, product, reduced.reshape(2 * q, 2 * q))
 
 

time: 66.1 us -> 49.7 us (0.75)
  local copies, waits for them, and re-layouts: 9.65 us -> 0 us
  Pallas kernels: 54.6 us -> 48.2 us
    unnamed x30 -> x0, local copies, waits for them, and re-layouts: 9.65 us -> none
    pallas_call x1, Pallas kernels: 51.2 us -> 43.8 us  [per_device(): pl.pallas_call(functools.partial(product_kernel, n_leaf, n_box, nb, width...]
    pallas_call x1, Pallas kernels: 3.38 us -> 4.4 us  [per_device(): pl.pallas_call(functools.partial(finish_kernel, float(panels)), out_shape...]
where the time goes in v2:
time: 49.7 us; the launch traced here: 49.5 us
  Pallas kernels  48.2 us (97%)
  between operations  1.29 us (3%)
    pallas_call x1, Pallas kernels, per_device(): pl.pallas_call(functools.partial(product_kernel, n_leaf, n_box, nb, width...  43.8 us
    pallas_call x1, Pallas kernels, per_device(): pl.pallas_call(functools.partial(finish_kernel, float(panels)), out_shape...  4.4 us

profile of v2, /device:TPU:0, one launch (start us, length us, event | category | flops | bytes accessed | tf_op | source)
XLA Modules:
  0.0 49.5 jit_solution(6181687025283454023)
XLA Ops:
  1.3 43.8 %shard_map.175 = (f32[64,1024]{1,0:T(8,128)}, f32[8,16,128]{2,1,0:T(8,128)}) custom-call(f32[64,1024]{1,0:T(8,128)} %k_ref.3, f32[32,1024]{1,0:T(8,128)} %b_ref.1, f32[3,1024]{1,0:T(4,128)} %pts_ref.1, f32[1,1024]{1,0:T(1,128)} %bitcast.8, f32[1,1024]{1,0:T(1,128)} %bitcast.9, s32[8,16]{1,0:T(8,128)} %near_ref.1, s32[8,12]{1,0:T(8,128)} %flist_ref.1, ...), custom_call_target="tpu_custom_call" | custom-call | tf_op jit(solution)/shard_map/pallas_call | solution.py:413
  45.1 4.4 %shard_map.176 = (f32[64,1024]{1,0:T(8,128)}, f32[64,64]{1,0:T(8,128)}, f32[64,64]{1,0:T(8,128)}) custom-call(f32[64,1024]{1,0:T(8,128)} %k_ref.3, f32[64,1024]{1,0:T(8,128)} %get-tuple-element.5.prod_ref, f32[128,128]{1,0:T(8,128)} %bitcast.7), custom_call_target="tpu_custom_call" | custom-call | tf_op jit(solution)/shard_map/pallas_call | solution.py:454

commit v3 on v2

--- a/solution.py
+++ b/solution.py
@@ -152,7 +152,7 @@
         kcat[i] = jnp.concatenate([high, rest], axis=0)
         return carry
 
-    lax.fori_loop(nb, 2 * nb, to_split, 0)
+    lax.fori_loop(nb, 2 * nb, to_split, 0, unroll=4)
     lane4 = lax.broadcasted_iota(jnp.int32, (r, 4 * r), 1) // r
     for c in range(cf_ref.shape[0]):
         tfine[c] = jnp.concatenate([cf_ref[c]] * 4, axis=1)
@@ -237,9 +237,9 @@
     def _():
         k_left.wait_recv()
 
-    lax.fori_loop(0, nb, to_split, 0)
-    lax.fori_loop(2 * nb, 3 * nb, to_split, 0)
-    lax.fori_loop(0, nb, near_box, 0)
+    lax.fori_loop(0, nb, to_split, 0, unroll=4)
+    lax.fori_loop(2 * nb, 3 * nb, to_split, 0, unroll=4)
+    lax.fori_loop(0, nb, near_box, 0, unroll=2)
 
     def open_fine(i, carry):
         for h in range(nb // 2):
@@ -248,7 +248,7 @@
             fpole[i * nb + 2 * h + 1] = rows[:, q:]
         return carry
 
-    lax.fori_loop(0, n_box, open_fine, 0)
+    lax.fori_loop(0, n_box, open_fine, 0, unroll=2)
 
     def open_coarse(i, carry):
         for h in range(n_leaf):
@@ -258,7 +258,7 @@
 
     for copy in leaf_out:
         copy.wait_recv()
-    lax.fori_loop(0, n_box, open_coarse, 0)
+    lax.fori_loop(0, n_box, open_coarse, 0, unroll=2)
 
     def coupled(table, class_of, pole, index_of, live, entries):
         left_side = []
@@ -291,7 +291,7 @@
         prod_ref[:, lanes] = prod_ref[:, lanes] + nn(local.T, b_ref[:, lanes])
         return carry
 
-    lax.fori_loop(0, nb, far_box, 0)
+    lax.fori_loop(0, nb, far_box, 0, unroll=4)
 
     stacked = jnp.concatenate([k_ref[...], prod_ref[...]], axis=0)
     gram = nt(stacked, stacked)

time: 49.7 us -> 48.8 us (0.982)
  Pallas kernels: 48.2 us -> 47.4 us
    pallas_call x1, Pallas kernels: 43.8 us -> 42.9 us  [per_device(): pl.pallas_call(functools.partial(product_kernel, n_leaf, n_box, nb, width...]
where the time goes in v3:
time: 48.8 us; the launch traced here: 48.7 us
  Pallas kernels  47.4 us (97%)
  between operations  1.29 us (3%)
    pallas_call x1, Pallas kernels, per_device(): pl.pallas_call(functools.partial(product_kernel, n_leaf, n_box, nb, width...  42.9 us
    pallas_call x1, Pallas kernels, per_device(): pl.pallas_call(functools.partial(finish_kernel, float(panels)), out_shape...  4.41 us

profile of v3, /device:TPU:0, one launch (start us, length us, event | category | flops | bytes accessed | tf_op | source)
XLA Modules:
  0.0 48.7 jit_solution(8223719112487084598)
XLA Ops:
  1.3 42.9 %shard_map.175 = (f32[64,1024]{1,0:T(8,128)}, f32[8,16,128]{2,1,0:T(8,128)}) custom-call(f32[64,1024]{1,0:T(8,128)} %k_ref.3, f32[32,1024]{1,0:T(8,128)} %b_ref.1, f32[3,1024]{1,0:T(4,128)} %pts_ref.1, f32[1,1024]{1,0:T(1,128)} %bitcast.8, f32[1,1024]{1,0:T(1,128)} %bitcast.9, s32[8,16]{1,0:T(8,128)} %near_ref.1, s32[8,12]{1,0:T(8,128)} %flist_ref.1, ...), custom_call_target="tpu_custom_call" | custom-call | tf_op jit(solution)/shard_map/pallas_call | solution.py:413
  44.2 4.4 %shard_map.176 = (f32[64,1024]{1,0:T(8,128)}, f32[64,64]{1,0:T(8,128)}, f32[64,64]{1,0:T(8,128)}) custom-call(f32[64,1024]{1,0:T(8,128)} %k_ref.3, f32[64,1024]{1,0:T(8,128)} %get-tuple-element.5.prod_ref, f32[128,128]{1,0:T(8,128)} %bitcast.7), custom_call_target="tpu_custom_call" | custom-call | tf_op jit(solution)/shard_map/pallas_call | solution.py:454

commit v4 on v3

--- a/solution.py
+++ b/solution.py
@@ -33,7 +33,7 @@
     k_ref, b_ref, pts_ref, size_ref, weight_ref,
     near_ref, flist_ref, fclass_ref, fcount_ref, clist_ref, cclass_ref, ccount_ref,
     cf_ref, cc_ref, up_ref, down_ref,
-    prod_ref, red_ref,
+    prod_ref, red_ref, own_ref,
     ext_k, ext_g, kcat, geo_t, greens, fbuf, lbuf, fpole, cpole, tfine, tcoarse, dloc,
     rbuf, rrecv, lrecv, gath,
     nk_s, nk_r, ng_s, ng_r, f_s, f_r, ff_s, ff_r, cl_s, cl_r,
@@ -126,6 +126,11 @@
     fbuf[box, fine_rows : fine_rows + r // 2, :] = jnp.concatenate(
         [cpole_own[: r // 2], cpole_own[r // 2 :]], axis=1
     )
+    own_gram = nt(k_ref[...], k_ref[...])
+    own_first = fine_rows + r // 2
+    fbuf[box, own_first : own_first + q // 2, :] = jnp.concatenate(
+        [own_gram[: q // 2], own_gram[q // 2 :]], axis=1
+    )
 
     def spread(buf, s_sems, r_sems, fs_sems, fr_sems):
         mine = buf.at[box]
@@ -219,6 +224,11 @@
         copy.wait_recv()
     for i in range(n_box):
         lbuf[leaf, i] = fbuf[i, fine_rows : fine_rows + r // 2, :]
+    own_sum = fbuf[0, own_first : own_first + q // 2, :]
+    for i in range(1, n_box):
+        own_sum = own_sum + fbuf[i, own_first : own_first + q // 2, :]
+    for i in range(q // r):
+        lbuf[leaf, n_box + i] = own_sum[i * (r // 2) : (i + 1) * (r // 2)]
     leaf_out = [
         remote(
             lbuf.at[leaf], lbuf.at[leaf], cl_s.at[d], cl_r.at[d],
@@ -259,6 +269,11 @@
     for copy in leaf_out:
         copy.wait_recv()
     lax.fori_loop(0, n_box, open_coarse, 0, unroll=2)
+    for i in range(q // r):
+        own_sum = lbuf[0, n_box + i]
+        for h in range(1, n_leaf):
+            own_sum = own_sum + lbuf[h, n_box + i]
+        own_ref[i * (r // 2) : (i + 1) * (r // 2), :] = own_sum
 
     def coupled(table, class_of, pole, index_of, live, entries):
         left_side = []
@@ -294,7 +309,8 @@
     lax.fori_loop(0, nb, far_box, 0, unroll=4)
 
     stacked = jnp.concatenate([k_ref[...], prod_ref[...]], axis=0)
-    gram = nt(stacked, stacked)
+    gram = nt(stacked, prod_ref[...])
+    gram = jnp.concatenate([gram[:q], gram[q:]], axis=1)
     share = rbuf.shape[1]
     for s in range(n_box):
         rbuf[s] = gram[s * share : (s + 1) * share]
@@ -348,13 +364,14 @@
         copy.wait_send()
 
 
-def finish_kernel(panels, k_ref, prod_ref, red_ref, basis_ref, hess_ref, factor_ref):
+def finish_kernel(panels, k_ref, prod_ref, red_ref, own_ref, basis_ref, hess_ref, factor_ref):
     q = k_ref.shape[0]
     red = red_ref[...]
-    basis_gram = red[:q, :q]
-    mixed = red[:q, q:]
-    mixed_t = red[q:, :q]
-    image = red[q:, q:]
+    own = own_ref[...]
+    basis_gram = jnp.concatenate([own[:, :q], own[:, q:]], axis=0)
+    mixed = red[:, :q]
+    mixed_t = mixed.T
+    image = red[:, q:]
     inverse = 1.0 / panels
     hess = mixed * inverse
     hess_t = mixed_t * inverse
@@ -405,29 +422,30 @@
     n_leaf = lax.axis_size("leaf")
     n_box = lax.axis_size("box")
     nz = n_box // 2
-    share = 2 * q // n_box
+    share = q // n_box
     panels = local * n_leaf * n_box
     vmem = pl.BlockSpec(memory_space=pltpu.VMEM)
     smem = pl.BlockSpec(memory_space=pltpu.SMEM)
     dma = lambda n: pltpu.SemaphoreType.DMA((n,))
-    product, reduced = pl.pallas_call(
+    product, reduced, own_gram = pl.pallas_call(
         functools.partial(
             product_kernel, n_leaf, n_box, nb, width, float(width * near_list.shape[1])
         ),
         out_shape=(
             jax.ShapeDtypeStruct((q, local), F32),
             jax.ShapeDtypeStruct((n_box, share, 2 * q), F32),
+            jax.ShapeDtypeStruct((q // 2, 2 * q), F32),
         ),
         in_specs=[vmem] * 5 + [smem] * 7 + [vmem] * 4,
-        out_specs=(vmem, vmem),
+        out_specs=(vmem, vmem, vmem),
         scratch_shapes=[
             pltpu.VMEM((3 * nb, q, width), F32),
             pltpu.VMEM((3 * nb, 8, width), F32),
             pltpu.VMEM((3 * nb, 2 * q, width), BF16),
             pltpu.VMEM((nb, width, 8), F32),
             pltpu.VMEM((nb * (near_list.shape[1] // 2), 2 * width, 2 * width), BF16),
-            pltpu.VMEM((n_box, nb // 2 * r + r // 2, 2 * q), F32),
-            pltpu.VMEM((n_leaf, n_box, r // 2, 2 * q), F32),
+            pltpu.VMEM((n_box, nb // 2 * r + r // 2 + q // 2, 2 * q), F32),
+            pltpu.VMEM((n_leaf, n_box + q // r, r // 2, 2 * q), F32),
             pltpu.VMEM((n_box * nb, r, q), F32),
             pltpu.VMEM((n_box * n_leaf, r, q), F32),
             pltpu.VMEM((couple_fine.shape[0], r, 4 * r), F32),
@@ -458,10 +476,10 @@
             jax.ShapeDtypeStruct((q, q), F32),
             jax.ShapeDtypeStruct((q, q), F32),
         ),
-        in_specs=[vmem] * 3,
+        in_specs=[vmem] * 4,
         out_specs=(vmem, vmem, vmem),
         compiler_params=pltpu.CompilerParams(vmem_limit_bytes=63 * 2**20),
-    )(krylov_block, product, reduced.reshape(2 * q, 2 * q))
+    )(krylov_block, product, reduced.reshape(q, 2 * q), own_gram)
 
 
 def solution(mesh):

time: 48.8 us -> 50.5 us (1.035)
  Pallas kernels: 47.4 us -> 49.1 us
    pallas_call x1, Pallas kernels: 42.9 us -> 44.7 us  [per_device(): pl.pallas_call(functools.partial(product_kernel, n_leaf, n_box, nb, width...]
where the time goes in v4:
time: 50.5 us; the launch traced here: 50.4 us
  Pallas kernels  49.1 us (97%)
  between operations  1.29 us (3%)
    pallas_call x1, Pallas kernels, per_device(): pl.pallas_call(functools.partial(product_kernel, n_leaf, n_box, nb, width...  44.7 us
    pallas_call x1, Pallas kernels, per_device(): pl.pallas_call(functools.partial(finish_kernel, float(panels)), out_shape...  4.35 us

profile of v4, /device:TPU:0, one launch (start us, length us, event | category | flops | bytes accessed | tf_op | source)
XLA Modules:
  0.0 50.4 jit_solution(15167567410708778437)
XLA Ops:
  1.3 44.7 %shard_map.175 = (f32[64,1024]{1,0:T(8,128)}, f32[8,8,128]{2,1,0:T(8,128)}, f32[32,128]{1,0:T(8,128)}) custom-call(f32[64,1024]{1,0:T(8,128)} %k_ref.3, f32[32,1024]{1,0:T(8,128)} %b_ref.1, f32[3,1024]{1,0:T(4,128)} %pts_ref.1, f32[1,1024]{1,0:T(1,128)} %bitcast.8, f32[1,1024]{1,0:T(1,128)} %bitcast.9, s32[8,16]{1,0:T(8,128)} %near_ref.1, ...), custom_call_target="tpu_custom_call" | custom-call | tf_op jit(solution)/shard_map/pallas_call | solution.py:430
  46.0 4.4 %shard_map.176 = (f32[64,1024]{1,0:T(8,128)}, f32[64,64]{1,0:T(8,128)}, f32[64,64]{1,0:T(8,128)}) custom-call(f32[64,1024]{1,0:T(8,128)} %k_ref.3, f32[64,1024]{1,0:T(8,128)} %get-tuple-element.6.prod_ref, f32[64,128]{1,0:T(8,128)} %bitcast.7, f32[32,128]{1,0:T(8,128)} %get-tuple-element.8.own_ref), custom_call_target="tpu_custom_call" | custom-call | tf_op jit(solution)/shard_map/pallas_call | solution.py:472

commit v5 on v3

--- a/solution.py
+++ b/solution.py
@@ -215,6 +215,17 @@
         fine_fwd[d - 1].start()
         if cuts[d + 1] > cuts[d]:
             lax.fori_loop(cuts[d], cuts[d + 1], green_box, 0)
+    @pl.when(box > 0)
+    def _():
+        k_right.wait_recv()
+
+    @pl.when(box < n_box - 1)
+    def _():
+        k_left.wait_recv()
+
+    lax.fori_loop(0, nb, to_split, 0, unroll=4)
+    lax.fori_loop(2 * nb, 3 * nb, to_split, 0, unroll=4)
+    lax.fori_loop(0, nb // 2, near_box, 0, unroll=2)
     for copy in [fine_out[0]] + fine_fwd:
         copy.wait_recv()
     for i in range(n_box):
@@ -228,18 +239,7 @@
     ]
     for copy in leaf_out:
         copy.start()
-
-    @pl.when(box > 0)
-    def _():
-        k_right.wait_recv()
-
-    @pl.when(box < n_box - 1)
-    def _():
-        k_left.wait_recv()
-
-    lax.fori_loop(0, nb, to_split, 0, unroll=4)
-    lax.fori_loop(2 * nb, 3 * nb, to_split, 0, unroll=4)
-    lax.fori_loop(0, nb, near_box, 0, unroll=2)
+    lax.fori_loop(nb // 2, nb, near_box, 0, unroll=2)
 
     def open_fine(i, carry):
         for h in range(nb // 2):

time: 48.8 us -> 50.1 us (1.027)
  Pallas kernels: 47.4 us -> 48.6 us
    pallas_call x1, Pallas kernels: 42.9 us -> 44.2 us  [per_device(): pl.pallas_call(functools.partial(product_kernel, n_leaf, n_box, nb, width...]
where the time goes in v5:
time: 50.1 us; the launch traced here: 49.9 us
  Pallas kernels  48.6 us (97%)
  between operations  1.29 us (3%)
    pallas_call x1, Pallas kernels, per_device(): pl.pallas_call(functools.partial(product_kernel, n_leaf, n_box, nb, width...  44.2 us
    pallas_call x1, Pallas kernels, per_device(): pl.pallas_call(functools.partial(finish_kernel, float(panels)), out_shape...  4.4 us

profile of v5, /device:TPU:0, one launch (start us, length us, event | category | flops | bytes accessed | tf_op | source)
XLA Modules:
  0.0 49.9 jit_solution(9496581299495328799)
XLA Ops:
  1.3 44.2 %shard_map.175 = (f32[64,1024]{1,0:T(8,128)}, f32[8,16,128]{2,1,0:T(8,128)}) custom-call(f32[64,1024]{1,0:T(8,128)} %k_ref.3, f32[32,1024]{1,0:T(8,128)} %b_ref.1, f32[3,1024]{1,0:T(4,128)} %pts_ref.1, f32[1,1024]{1,0:T(1,128)} %bitcast.8, f32[1,1024]{1,0:T(1,128)} %bitcast.9, s32[8,16]{1,0:T(8,128)} %near_ref.1, s32[8,12]{1,0:T(8,128)} %flist_ref.1, ...), custom_call_target="tpu_custom_call" | custom-call | tf_op jit(solution)/shard_map/pallas_call | solution.py:413
  45.5 4.4 %shard_map.176 = (f32[64,1024]{1,0:T(8,128)}, f32[64,64]{1,0:T(8,128)}, f32[64,64]{1,0:T(8,128)}) custom-call(f32[64,1024]{1,0:T(8,128)} %k_ref.3, f32[64,1024]{1,0:T(8,128)} %get-tuple-element.5.prod_ref, f32[128,128]{1,0:T(8,128)} %bitcast.7), custom_call_target="tpu_custom_call" | custom-call | tf_op jit(solution)/shard_map/pallas_call | solution.py:454
